TPU v7x, 128 devices: a whole 4x4x4 slice. The times are simulated.
128 devices in a mesh: seq: 16 (over y_lo, z, core), kvh: 8 (over y_hi, x).
Axes of the slice: x: 4, y: 4 (y_hi: 2, y_lo: 2; y = y_hi * 2 + y_lo), z: 4, core: 2. Of those that a mesh axis runs over, the one named last changes fastest.
Arguments:
- hidden_in: bfloat16 [8192, 8192], P('seq', 'kvh'), may hold values from -10 to 10
- queries: bfloat16 [8192, 4096], P('seq', 'kvh'), may hold values from -8 to 8
- keys: bfloat16 [8192, 1024], P('seq', 'kvh'), may hold values from -12 to 12
- values: bfloat16 [8192, 1024], P('seq', 'kvh'), may hold values from -12 to 12
- out_weight: bfloat16 [4096, 8192], P('kvh'), may hold values from -0.09375 to 0.09375
- norm_gain: float32 [8192], replicated, may hold values from 0.1 to 1.9
- head_weight: bfloat16 [81920, 8192], P(('seq', 'kvh')), may hold values from -5 to 5
- caption_pos: int32 [256], replicated, may hold values from 0 to 8191, as said below
- targets: int32 [256], replicated, may hold values from 0 to 81919
Outputs:
- layer_out: bfloat16 [8192, 8192], P('seq', 'kvh')
- log_probs: float32 [256], replicated
Inputs may be any that keep to these rules, and one draw needn't show every extreme that they name: `caption_pos`: positions increase; exactly one lies in each aligned run of 32 positions; the first is 0 and the last is 8191.
All inputs are finite; a program needn't handle non-finite values.
Results may differ from a plain program's by a relative error of at most 0.015.
Values may be sent and summed in bfloat16 or wider, within the bound.
A program may use at most 128 MiB of HBM per device.

v0:
```python
import jax
import jax.numpy as jnp
from jax import lax
from jax.sharding import PartitionSpec as P


def empty_state(heads, half_rows, head_dim):
    return (
        jnp.full((heads, half_rows), -1e30, jnp.float32),
        jnp.zeros((heads, half_rows), jnp.float32),
        jnp.zeros((heads, half_rows, head_dim), jnp.float32),
    )


def attend_block(states, query, query_start, key_rows, value_rows, key_start):
    half_rows = query.shape[0]
    head_dim = key_rows.shape[1]
    heads = query.shape[1] // head_dim
    key_count = key_rows.shape[0]

    def update(carried):
        running_max, totals, accumulated = carried
        shaped = query.reshape(half_rows, heads, head_dim)
        scores = jnp.einsum(
            "rhd,kd->hrk", shaped, key_rows, preferred_element_type=jnp.float32
        ) * head_dim ** (-0.5)
        query_position = query_start + jnp.arange(half_rows)
        key_position = key_start + jnp.arange(key_count)
        allowed = key_position[None, :] <= query_position[:, None]
        scores = jnp.where(allowed[None], scores, -1e30)
        new_max = jnp.maximum(running_max, jnp.max(scores, axis=2))
        weights = jnp.exp(scores - new_max[:, :, None])
        factor = jnp.exp(running_max - new_max)
        totals = totals * factor + jnp.sum(weights, axis=2)
        product = jnp.einsum(
            "hrk,kd->hrd",
            weights.astype(jnp.bfloat16),
            value_rows,
            preferred_element_type=jnp.float32,
        )
        accumulated = accumulated * factor[:, :, None] + product
        return (new_max, totals, accumulated)

    return lax.cond(key_start <= query_start + half_rows - 1, update, lambda kept: kept, states)


def attend(states, query, query_start, key_piece, value_piece, key_block):
    key_count = key_piece.shape[0]
    steps_count = key_count // key_block
    stacked_keys = key_piece.reshape(steps_count, key_block, key_piece.shape[1])
    stacked_values = value_piece.reshape(steps_count, key_block, value_piece.shape[1])

    def step_block(carried, inputs):
        key_rows, value_rows, position = inputs
        return (
            attend_block(carried, query, query_start, key_rows, value_rows, position * key_block),
            None,
        )

    result, unused = lax.scan(
        step_block, states, (stacked_keys, stacked_values, jnp.arange(steps_count))
    )
    return result


def finish(states):
    running_max, totals, accumulated = states
    heads, half_rows, head_dim = accumulated.shape
    result = accumulated / totals[:, :, None]
    return (
        jnp.transpose(result, (1, 0, 2)).reshape(half_rows, heads * head_dim).astype(jnp.bfloat16)
    )


def body(
    hidden_in, queries, keys, values, out_weight, norm_gain, head_weight, caption_pos, targets
):
    seq_count = lax.axis_size("seq")
    seq_index = lax.axis_index("seq")
    row_count = queries.shape[0]
    half_rows = row_count // 2
    head_dim = keys.shape[1]
    heads = queries.shape[1] // head_dim
    own_start = seq_index * row_count
    query_low = queries[:half_rows]
    query_high = queries[half_rows:]
    high_start = own_start + half_rows
    initial = (empty_state(heads, half_rows, head_dim), empty_state(heads, half_rows, head_dim))
    pieces = (
        lax.all_gather(keys, "seq", axis=0, tiled=True),
        lax.all_gather(values, "seq", axis=0, tiled=True),
    )
    low_state = attend(initial[0], query_low, own_start, pieces[0], pieces[1], row_count)
    high_state = attend(initial[1], query_high, high_start, pieces[0], pieces[1], row_count)
    attended_low = finish(low_state)
    attended_high = finish(high_state)
    attended = jnp.concatenate([attended_low, attended_high], axis=0)
    projected = jnp.dot(attended, out_weight, preferred_element_type=jnp.float32)
    per_device = caption_pos.shape[0] // seq_count
    local_spots = (
        lax.dynamic_slice_in_dim(caption_pos, seq_index * per_device, per_device) - own_start
    )
    summed_share = lax.psum_scatter(
        projected.astype(jnp.bfloat16), "kvh", scatter_dimension=1, tiled=True
    ).astype(jnp.float32)
    layer_local = (hidden_in.astype(jnp.float32) + summed_share).astype(jnp.bfloat16)
    caption_piece = jnp.take(layer_local, local_spots, axis=0)
    gathered = lax.all_gather(caption_piece, "kvh", axis=1, tiled=True)
    gain_row = norm_gain[None, :]
    widened = lax.all_gather(gathered, "seq", axis=0, tiled=True).astype(jnp.float32)
    mean_square = jnp.mean(widened * widened, axis=1, keepdims=True)
    normed = (widened * lax.rsqrt(mean_square + 1e-06) * gain_row).astype(jnp.bfloat16)
    logits = lax.dot_general(
        normed, head_weight, (((1,), (1,)), ((), ())), preferred_element_type=jnp.float32
    )
    vocab_count = head_weight.shape[0]
    vocab_start = lax.axis_index(("seq", "kvh")) * vocab_count
    entry_ids = vocab_start + jnp.arange(vocab_count, dtype=jnp.int32)
    own_target = jnp.sum(jnp.where(targets[:, None] == entry_ids[None, :], logits, 0.0), axis=1)
    local_max = jnp.max(logits, axis=1)
    top_logit = lax.pmax(local_max, ("seq", "kvh"))
    local_total = jnp.sum(jnp.exp(logits - top_logit[:, None]), axis=1)
    exp_total, picked = lax.psum((local_total, own_target), ("seq", "kvh"))
    log_probs = picked - (top_logit + jnp.log(exp_total))
    return (layer_local, log_probs)


def solution(mesh):
    in_specs = (
        P("seq", "kvh"),
        P("seq", "kvh"),
        P("seq", "kvh"),
        P("seq", "kvh"),
        P("kvh", None),
        P(),
        P(("seq", "kvh"), None),
        P(),
        P(),
    )
    out_specs = (P("seq", "kvh"), P())
    return jax.shard_map(body, mesh=mesh, in_specs=in_specs, out_specs=out_specs, check_vma=False)
```

profile of v0, /device:TPU:1, one launch (start us, length us, event | category | flops | bytes accessed | tf_op | source)
XLA Modules:
  0.0 581.5 jit_solution(4175177041000686541)
XLA Ops:
  7.2 0.7 all-gather.4.cloned.1.call-update
  7.9 0.7 all-gather.6.cloned.1.call-update
  8.7 1.1 fusion.37
  9.8 38.0 %all-gather.4.cloned.1.call-done = bf16[8192,128]{1,0:T(8,128)(2,1)} async-done(((bf16[512,128]{1,0:T(8,128)(2,1)}), bf16[8192,128]{1,0:T(8,128)(2,1)}) %all-gather.4.cloned.1.call-update) | async-done | bytes 2097168 | tf_op jit(solution)/shard_map/all_gather | solution.py:90
  47.7 35.8 %all-gather.6.cloned.1.call-done = bf16[8192,128]{1,0:T(8,128)(2,1)} async-done(((bf16[512,128]{1,0:T(8,128)(2,1)}), bf16[8192,128]{1,0:T(8,128)(2,1)}) %all-gather.6.cloned.1.call-update) | async-done | bytes 2097168 | tf_op jit(solution)/shard_map/all_gather | solution.py:91
  83.5 27.5 %while.32 = (s32[]{:T(128)}, f32[4,256]{1,0:T(4,128)S(1)}, f32[4,256]{1,0:T(4,128)S(1)}, f32[4,256,128]{2,1,0:T(8,128)S(1)}, s32[16]{0:T(128)S(1)}, /*index=5*/s...) while((s32[]{:T(128)}, f32[4,256]{1,0:T(4,128)S(1)}, ...), condition=%wide.region_5.6_spmd, body=%wide.region_0.5_spmd.sunk | while | flops 272501504 | bytes 8199459 | solution.py:60
  83.6 0.6 dynamic_slice.76
  84.8 3.6 conditional.4
  85.0 1.4 fusion.35
  86.7 1.6 convolution_add_fusion
  88.4 0.6 dynamic_slice.76
  89.6 3.6 conditional.4
  89.8 1.4 fusion.35
  91.5 1.6 convolution_add_fusion
  93.2 0.6 dynamic_slice.76
  94.5 0.6 dynamic_slice.76
  95.7 0.6 dynamic_slice.76
  97.0 0.6 dynamic_slice.76
  98.3 0.6 dynamic_slice.76
  99.6 0.6 dynamic_slice.76
  100.8 0.6 dynamic_slice.76
  102.1 0.6 dynamic_slice.76
  103.4 0.6 dynamic_slice.76
  104.7 0.6 dynamic_slice.76
  105.9 0.6 dynamic_slice.76
  107.2 0.6 dynamic_slice.76
  108.5 0.6 dynamic_slice.76
  109.8 0.6 dynamic_slice.76
  111.3 27.5 %while.33 = (s32[]{:T(128)}, f32[4,256]{1,0:T(4,128)S(1)}, f32[4,256]{1,0:T(4,128)S(1)}, f32[4,256,128]{2,1,0:T(8,128)S(1)}, s32[16]{0:T(128)S(1)}, /*index=5*/s...) while((s32[]{:T(128)}, f32[4,256]{1,0:T(4,128)S(1)}, ...), condition=%wide.region_11.12_spmd, body=%wide.region_6.11_spmd.sunk | while | flops 272501504 | bytes 8199459 | solution.py:60
  111.3 0.6 dynamic_slice.77
  112.6 3.6 conditional.5
  112.8 1.4 fusion.36
  114.5 1.6 convolution_add_fusion.1
  117.4 3.6 conditional.5
  117.6 1.4 fusion.36
  119.3 1.6 convolution_add_fusion.1
  127.3 0.6 dynamic_slice.77
  128.6 0.6 dynamic_slice.77
  129.9 0.6 dynamic_slice.77
  139.1 10.2 %convolution_convert_fusion = bf16[512,8192]{1,0:T(8,128)(2,1)} fusion(bf16[512,8192]{1,0:T(8,128)(2,1)} %param.21, bf16[256,512]{0,1:T(8,128)(2,1)S(1)} %bitcast.59, bf16[256,512]{0,1:T(8,128)(2,1)S(1)} %bitcast.58), kind=kOutput, calls=%fused_computation.39 | convolution fusion | flops 4300210176 | bytes 17301504 | tf_op jit(solution)/shard_map/dot_general | solution.py:98
  150.1 211.2 %reduce-scatter.2.cloned.1.call-done = bf16[512,1024]{1,0:T(8,128)(2,1)} async-done(((bf16[512,8192]{1,0:T(8,128)(2,1)}), bf16[512,1024]{1,0:T(8,128)(2,1)}) %reduce-scatter.2.cloned.1.call-update) | async-done | bytes 1048592 | tf_op jit(solution)/shard_map/reduce_scatter | solution.py:103
  361.3 1.6 add_convert_fusion
  363.6 30.0 %all_gather.14 = bf16[16,8192]{1,0:T(8,128)(2,1)} all-gather(bf16[16,1024]{1,0:T(8,128)(2,1)S(1)} %broadcast_select_fusion), channel_id=1, replica_groups=mesh['seq'=16,'kvh'=8] {'kvh'}, dimensions={1}, use_global_device_ids=true | all-gather | bytes 294912 | tf_op jit(solution)/shard_map/all_gather | solution.py:108
  393.7 42.2 %all-gather.8.cloned.1.call-done = bf16[256,8192]{1,0:T(8,128)(2,1)} async-done(((bf16[16,8192]{1,0:T(8,128)(2,1)}), bf16[256,8192]{1,0:T(8,128)(2,1)}) %all-gather.8.cloned.1.call-update) | async-done | bytes 4194320 | tf_op jit(solution)/shard_map/all_gather | solution.py:110
  435.9 3.3 fusion.24
  439.4 6.4 %fusion.38 = (f32[256]{0:T(256)S(1)}, f32[256,640]{1,0:T(8,128)S(1)}) fusion(bf16[640,8192]{1,0:T(8,128)(2,1)} %param.23, bf16[256,8192]{1,0:T(8,128)(2,1)S(1)} %copy-done, f32[8192]{0:T(1024)S(1)} %copy-done.5, f32[256]{0:T(256)S(1)} %add_rsqrt_fusion), kind=kOutput, calls=%fused_computation.67 | convolution fusion | flops 2692906752 | bytes 15370240 | tf_op jit(solution)/shard_map/dot_general | solution.py:113
  445.8 64.8 %pmax.7 = f32[256]{0:T(256)S(1)} all-reduce(f32[256]{0:T(256)S(1)} %get-tuple-element.458), channel_id=1, replica_groups=mesh['seq'=16,'kvh'=8] {'seq','kvh'}, use_global_device_ids=true, to_apply=%region_17.18 | all-reduce | flops 256 | bytes 2048 | tf_op jit(solution)/shard_map/pmax | solution.py:121
  510.9 63.5 %all-reduce = (f32[256]{0:T(256)S(1)}, f32[256]{0:T(256)S(1)}) all-reduce(f32[256]{0:T(256)S(1)} %get-tuple-element.403, f32[256]{0:T(256)S(1)} %get-tuple-element.402), channel_id=1, replica_groups=mesh['seq'=16,'kvh'=8] {'seq','kvh'}, use_global_device_ids=true, to_apply=%region_15.16 | all-reduce | flops 512 | bytes 4096 | tf_op jit(solution)/shard_map/psum | solution.py:123
  (106 shorter events, 12.9 us)
Async XLA Ops:
  7.2 40.6 %all-gather.4.cloned.1.call-start = ((), (), s32[]{:S(2)}) async-start(), calls=%async_computation.1 | async-start | bytes 2228224 | tf_op jit(solution)/shard_map/all_gather | solution.py:90
  7.9 75.6 %all-gather.6.cloned.1.call-start = ((), (), s32[]{:S(2)}) async-start(), calls=%async_computation.2 | async-start | bytes 2228224 | tf_op jit(solution)/shard_map/all_gather | solution.py:91
  8.6 352.6 %reduce-scatter.2.cloned.1.call-start = ((), (), s32[]{:S(2)}) async-start(), calls=%async_computation.3 | async-start | bytes 9437184 | tf_op jit(solution)/shard_map/reduce_scatter | solution.py:103
  149.3 0.7 copy-start.4
  149.3 212.0 %copy-start.2 = (bf16[512,1024]{1,0:T(8,128)(2,1)S(1)}, bf16[512,1024]{1,0:T(8,128)(2,1)}, u32[]{:S(2)}) copy-start(bf16[512,1024]{1,0:T(8,128)(2,1)} %param.17) | copy-start | bytes 3145732
  149.3 286.6 %all-gather.8.cloned.1.call-start = ((), (), s32[]{:S(2)}) async-start(), calls=%async_computation.4 | async-start | bytes 4456448 | tf_op jit(solution)/shard_map/all_gather | solution.py:110
  361.3 77.9 %copy-start.5 = (f32[8192]{0:T(1024)S(1)}, f32[8192]{0:T(1024)}, u32[]{:S(2)}) copy-start(f32[8192]{0:T(1024)} %param.22) | copy-start | bytes 98308
  362.9 76.3 %copy-start.1 = (bf16[512,1024]{1,0:T(8,128)(2,1)}, bf16[512,1024]{1,0:T(8,128)(2,1)S(1)}, u32[]{:S(2)}) copy-start(bf16[512,1024]{1,0:T(8,128)(2,1)S(1)} %add_convert_fusion) | copy-start | bytes 3145732
  435.9 3.4 copy-start
  439.4 71.2 %copy-start.3 = (s32[256]{0:T(256)S(1)}, s32[256]{0:T(256)}, u32[]{:S(2)}) copy-start(s32[256]{0:T(256)} %param.25) | copy-start | bytes 3076
Sparse Core Ops, SparseCore 0:
  9.7 37.9 all-gather.3
  49.4 34.0 all-gather.5
  149.5 211.7 reduce-scatter.1
  393.8 42.0 all-gather.7
where the time goes:
time: 583 us; the launch traced here: 582 us
  waiting for transfers between devices  329 us (56%)
  blocking collectives  158 us (27%)
  matrix products  28.7 us (5%)
  local copies, waits for them, and re-layouts  22.7 us (4%)
  loops' own time  21.2 us (4%)
  between operations  13.9 us (2%)
  other arithmetic  7.9 us (1%)
    reduce_scatter x1, waiting for transfers between devices, body(): lax.psum_scatter(projected.astype(jnp.bfloat16), 'kvh', scatter_dimension...  211 us
    pmax x1, blocking collectives, body(): top_logit = lax.pmax(local_max, ('seq', 'kvh'))  64.8 us
    psum x1, blocking collectives, body(): exp_total, picked = lax.psum((local_total, own_target), ('seq', 'kvh'))  63.5 us
    all_gather x1, waiting for transfers between devices, body(): lax.all_gather(gathered, 'seq', axis=0, tiled=True).astype(jnp.float32)  42.2 us
    all_gather x1, waiting for transfers between devices, body(): lax.all_gather(keys, 'seq', axis=0, tiled=True)  38 us
    all_gather x1, waiting for transfers between devices, body(): lax.all_gather(values, 'seq', axis=0, tiled=True)  35.8 us
    all_gather x1, blocking collectives, body(): gathered = lax.all_gather(caption_piece, 'kvh', axis=1, tiled=True)  30 us
    another operation x2, loops' own time, attend(): lax.scan(step_block, states, (stacked_keys, stacked_values, jnp.arange(st...  20.6 us
  transfers between devices with their start and end apart: 4, of which 4 were waited for; matrix products, arithmetic and copies ran while one was open for 0% of the time, Pallas kernels for 0%

commit v1 on v0

v1 whole, which is shorter than its diff:
```python
import functools
import jax
import jax.numpy as jnp
from jax import lax
from jax.experimental import pallas as pl
from jax.experimental.pallas import tpu as pltpu
from jax.sharding import PartitionSpec as P

MESH = pl.DeviceIdType.MESH
F32 = jnp.float32
BF16 = jnp.bfloat16
NT = (((1,), (1,)), ((), ()))
NEG = -1e30
SEQ = 16
KVH = 8
PAIRS = 8
XS = 4
TOK = 512
HD = 128
HEADS = 4
RB = 128
NRB = TOK // RB
CAPS = 16
NCAP = SEQ * CAPS
FEAT = 1024
VOC = 640
SCALE = HD ** (-0.5)
SCALE2 = SCALE * 1.4426950408889634


def rcopy(src, dst, send_sem, recv_sem, device):
    return pltpu.make_async_remote_copy(
        src_ref=src,
        dst_ref=dst,
        send_sem=send_sem,
        recv_sem=recv_sem,
        device_id=device,
        device_id_type=MESH,
    )


def kernel(
    q_ref, k_ref, v_ref, hid_ref, ow_ref, gain_ref, hw_ref, cap_ref, tgt_ref,
    out_ref, lp_ref,
    kv, m_s, acc_s, wbuf, hw, call, ncap, abuf, psend, precv, lacc,
    cq, cpo, cpi, cro, cri, logit, stat, st1, st2,
    wl_m, wo_m, hw_m, kv_s, kv_r, kf_s, kf_r, w_s, w_r, wf_s, wf_r,
    cq_s, cq_r, cp_s, cp_r, cr_s, cr_r, ck_s, ck_r, cs_s, cs_r, cf_s, cf_r,
    a_s, a_r, y_s, y_r, s1_s, s1_r, s2_s, s2_r,
):
    s = lax.axis_index("seq")
    k = lax.axis_index("kvh")
    pair, core = lax.div(s, 2), lax.rem(s, 2)
    yhi, x = lax.div(k, XS), lax.rem(k, XS)
    other_y = 1 - yhi
    sib = (2 * pair + 1 - core, k)
    y_dev = (s, other_y * XS + x)

    def pair_dev(p):
        return (2 * p + core, k)

    def x_dev(xx):
        return (s, yhi * XS + xx)

    def cols(kk):
        return pl.ds(pl.multiple_of(kk * FEAT, FEAT), FEAT)

    half = pl.ds(pl.multiple_of(core * TOK, TOK), TOK)
    whalf = pl.ds(pl.multiple_of(core * 256, 256), 256)

    own_w = [
        pltpu.make_async_copy(ow_ref.at[:, cols(y * XS + x)], wbuf.at[y, x], wo_m.at[y])
        for y in range(2)
    ]
    local_w = [
        pltpu.make_async_copy(ow_ref.at[:, cols(i)], hw.at[0:TOK, cols(i)], wl_m.at[i])
        for i in range(KVH)
    ]
    head_copy = pltpu.make_async_copy(hw_ref, hw, hw_m.at[0])
    barrier = pltpu.get_barrier_semaphore()
    for j in range(1, SEQ):
        pl.semaphore_signal(barrier, inc=1, device_id=(lax.rem(s + j, SEQ), k), device_id_type=MESH)
    for j in range(1, KVH):
        pl.semaphore_signal(barrier, inc=1, device_id=(s, lax.rem(k + j, KVH)), device_id_type=MESH)
    for c in local_w + own_w:
        c.start()
    kv[pair, half, 0:HD] = k_ref[...]
    kv[pair, half, HD : 2 * HD] = v_ref[...]
    own_rows = pl.ds(pl.multiple_of(s * 64, 64), CAPS)
    spots = cap_ref[own_rows, :] - s * TOK
    sel = (lax.broadcasted_iota(jnp.int32, (CAPS, TOK), 1) == spots).astype(F32).astype(BF16)
    for h in range(HEADS):
        picked = jnp.dot(sel, q_ref[:, h * HD : (h + 1) * HD], preferred_element_type=F32)
        cq[s, h * CAPS : (h + 1) * CAPS, :] = picked.astype(BF16)
    pl.semaphore_wait(barrier, SEQ - 1 + KVH - 1)

    def cq_copy(j):
        return rcopy(cq.at[s], cq.at[s], cq_s.at[j], cq_r.at[s], (j, k))

    def start_cq(j, carry):
        cq_copy(j).start()
        return carry

    lax.fori_loop(0, s, start_cq, 0)

    def kv_copy(j):
        block = kv.at[pair, half]
        return rcopy(block, block, kv_s.at[j], kv_r.at[pair], pair_dev(pair + j))

    def kf_copy(p):
        block = kv.at[p, half]
        return rcopy(block, block, kf_s.at[p], kf_r.at[p], sib)

    kf_copy(pair).start()
    for j in range(1, PAIRS):
        pl.when(pair + j < PAIRS)(lambda j=j: kv_copy(j).start())

    def w_copy(j, y):
        xx = lax.rem(x + j, XS)
        return rcopy(
            ow_ref.at[whalf, cols(y * XS + xx)], wbuf.at[y, x, whalf], w_s.at[y, j], w_r.at[y, x], x_dev(xx)
        )

    for j in range(1, XS):
        for y in range(2):
            w_copy(j, y).start()

    ones = jnp.ones((2 * TOK, HD), BF16)

    def attend(rb, p, own):
        rows = pl.ds(pl.multiple_of(rb * RB, RB), RB)
        keys = kv[p, :, 0:HD]
        vals = jnp.concatenate([kv[p, :, HD : 2 * HD], ones], axis=1)
        if own:
            row_at = lax.broadcasted_iota(jnp.int32, (RB, 2 * TOK), 0) + (core * TOK + rb * RB)
            allowed = lax.broadcasted_iota(jnp.int32, (RB, 2 * TOK), 1) <= row_at
        for h in range(HEADS):
            at = rb * HEADS + h
            query = q_ref[rows, h * HD : (h + 1) * HD]
            sc = lax.dot_general(query, keys, NT, preferred_element_type=F32)
            if own:
                sc = jnp.where(allowed, sc, NEG)
                top = jnp.broadcast_to(jnp.max(sc, axis=1, keepdims=True), (RB, HD))
            else:
                old = m_s[at]
                top = jnp.maximum(old, jnp.max(sc, axis=1, keepdims=True))
            w = jnp.exp2((sc - top[:, 0:1]) * SCALE2).astype(BF16)
            m_s[at] = top
            pv = jnp.dot(w, vals, preferred_element_type=F32)
            if own:
                acc_s[at] = pv
            else:
                f = jnp.exp2((old - top) * SCALE2)
                acc_s[at] = acc_s[at] * jnp.concatenate([f, f], axis=1) + pv

    def attend_all(p, own):
        def step(rb, carry):
            attend(rb, p, own)
            return carry

        lax.fori_loop(0, NRB, step, 0)

    def half_arrived(j):
        p = pair - j
        block = kv.at[p, half]
        rcopy(block, block, kv_s.at[0], kv_r.at[p], sib).wait_recv()
        kf_copy(p).start()

    def sib_arrived(p):
        block = kv.at[p, half]
        rcopy(block, block, kf_s.at[p], kf_r.at[p], sib).wait_recv()

    sib_arrived(pair)
    attend_all(pair, True)
    pl.when(pair >= 1)(lambda: half_arrived(1))

    def wait_cq(j, carry):
        rcopy(cq.at[j], cq.at[j], cq_s.at[j], cq_r.at[j], sib).wait_recv()
        return carry

    lax.fori_loop(s + 1, SEQ, wait_cq, 0)
    own_vals = jnp.concatenate([v_ref[...], jnp.ones((TOK, HD), BF16)], axis=1)
    lane = lax.broadcasted_iota(jnp.int32, (TOK, HD), 1)
    for g in range(2):
        queries = cq[g * 8 : (g + 1) * 8].reshape(TOK, HD)
        sc = lax.dot_general(queries, k_ref[...], NT, preferred_element_type=F32)
        key_at = lax.broadcasted_iota(jnp.int32, (TOK, TOK), 1) + s * TOK
        sc = jnp.where(key_at <= cap_ref[g * TOK : (g + 1) * TOK, :], sc, NEG)
        top = jnp.broadcast_to(jnp.max(sc, axis=1, keepdims=True), (TOK, HD))
        w = jnp.exp2((sc - top[:, 0:1]) * SCALE2).astype(BF16)
        pv = jnp.dot(w, own_vals, preferred_element_type=F32)
        total = pv[:, HD:]
        lse = top * SCALE + jnp.log(total)
        hi = lse.astype(BF16).astype(F32)
        mid = (lse - hi).astype(BF16).astype(F32)
        low = lse - hi - mid
        parts = jnp.where(lane < 32, hi, jnp.where(lane < 64, mid, low))
        both = jnp.concatenate([pv[:, :HD] / total, parts], axis=1).astype(BF16)
        cpo[g * 8 : (g + 1) * 8] = both.reshape(8, 64, 2 * HD)

    def cp_copy(j):
        return rcopy(cpo.at[j], cpi.at[s], cp_s.at[j], cp_r.at[s], (j, k))

    def start_cp(j, carry):
        cp_copy(j).start()
        return carry

    lax.fori_loop(s + 1, SEQ, start_cp, 0)

    def phase_one(j):
        pl.when(pair >= j + 1)(lambda: half_arrived(j + 1))

        def work():
            sib_arrived(pair - j)
            attend_all(pair - j, False)

        pl.when(pair >= j)(work)

    phase_one(1)

    def unpack(block):
        t = block[:, HD:].astype(F32)
        return block[:, :HD].astype(F32), t[:, 0:1] + t[:, 32:33] + t[:, 64:65]

    def combine(j, carry):
        top, total, acc = carry
        rcopy(cpi.at[j], cpi.at[j], cp_s.at[j], cp_r.at[j], sib).wait_recv()
        o, lse = unpack(cpi[j])
        new = jnp.maximum(top, lse)
        a, b = jnp.exp(top - new), jnp.exp(lse - new)
        return new, total * a + b, acc * a + o * b

    own_o, own_lse = unpack(cpo[s])
    top, total, acc = lax.fori_loop(0, s, combine, (own_lse, jnp.ones((64, 1), F32), own_o))
    att = acc / total
    att = jnp.concatenate([att[h * CAPS : (h + 1) * CAPS] for h in range(HEADS)], axis=1).astype(BF16)
    for i in range(KVH):
        local_w[i].wait()
        cro[i] = jnp.dot(att, hw[0:TOK, i * FEAT : (i + 1) * FEAT], preferred_element_type=F32).astype(BF16)

    def cr_copy(j):
        kk = lax.rem(k + j, KVH)
        return rcopy(cro.at[kk], cri.at[k], cr_s.at[j], cr_r.at[k], (s, kk))

    for j in range(1, KVH):
        cr_copy(j).start()
    head_copy.start()

    phase_one(2)

    cap_sum = cro[k].astype(F32) + jnp.dot(sel, hid_ref[...], preferred_element_type=F32)
    for j in range(1, KVH):
        kk = lax.rem(k + j, KVH)
        rcopy(cri.at[kk], cri.at[kk], cr_s.at[0], cr_r.at[kk], sib).wait_recv()
        cap_sum = cap_sum + cri[kk].astype(F32)

    def cap_rows(ss):
        return pl.ds(pl.multiple_of(ss * CAPS, CAPS), CAPS)

    call[k, cap_rows(s), :] = cap_sum.astype(BF16)

    def ck_copy(j):
        block = call.at[k, cap_rows(s)]
        return rcopy(block, block, ck_s.at[j], ck_r.at[k], (s, lax.rem(k + j, KVH)))

    for j in range(1, KVH):
        ck_copy(j).start()

    phase_one(3)

    for j in range(1, KVH):
        kk = lax.rem(k + j, KVH)
        block = call.at[kk, cap_rows(s)]
        rcopy(block, block, ck_s.at[0], ck_r.at[kk], sib).wait_recv()

    def cs_copy(j):
        block = call.at[:, cap_rows(s)]
        return rcopy(block, block, cs_s.at[j], cs_r.at[pair], pair_dev(lax.rem(pair + j, PAIRS)))

    def cf_copy(p):
        block = call.at[:, cap_rows(2 * p + core)]
        return rcopy(block, block, cf_s.at[p], cf_r.at[p], sib)

    cf_copy(pair).start()
    for j in range(1, PAIRS):
        cs_copy(j).start()

    for j in range(4, PAIRS):
        if j + 1 < PAIRS:
            pl.when(pair >= j + 1)(lambda j=j: half_arrived(j + 1))
        pl.when(pair >= j)(lambda j=j: sib_arrived(pair - j))

    def a_copy(rb, j):
        block = abuf.at[rb, x]
        return rcopy(block, block, a_s.at[rb, j], a_r.at[rb, x], x_dev(lax.rem(x + j, XS)))

    def finish(rb):
        def step(j, carry):
            attend(rb, pair - j, False)
            return carry

        lax.fori_loop(4, pair + 1, step, 0)
        for h in range(HEADS):
            done = acc_s[rb * HEADS + h]
            abuf[rb, x, :, h * HD : (h + 1) * HD] = (done[:, :HD] / done[:, HD:]).astype(BF16)
        for j in range(1, XS):
            a_copy(rb, j).start()

    def y_copy(rb):
        return rcopy(psend.at[rb], precv.at[rb], y_s.at[rb], y_r.at[rb], y_dev)

    def project(rb):
        for j in range(1, XS):
            xx = lax.rem(x + j, XS)
            block = abuf.at[rb, xx]
            rcopy(block, block, a_s.at[rb, 0], a_r.at[rb, xx], sib).wait_recv()

        def product(y):
            parts = [jnp.dot(abuf[rb, xx], wbuf[y, xx], preferred_element_type=F32) for xx in range(XS)]
            return (parts[0] + parts[1]) + (parts[2] + parts[3])

        psend[rb] = product(other_y).astype(BF16)
        y_copy(rb).start()
        lacc[rb] = product(yhi) + hid_ref[rb * RB : (rb + 1) * RB, :].astype(F32)

    def w_arrived():
        for c in own_w:
            c.wait()
        for j in range(1, XS):
            xx = lax.rem(x + j, XS)
            for y in range(2):
                block = wbuf.at[y, xx, whalf]
                rcopy(block, block, w_s.at[y, 0], w_r.at[y, xx], sib).wait_recv()
                wf_copy(j, y).start()
        for j in range(1, XS):
            xx = lax.rem(x + j, XS)
            for y in range(2):
                block = wbuf.at[y, xx, whalf]
                rcopy(block, block, wf_s.at[y, xx], wf_r.at[y, xx], sib).wait_recv()

    def wf_copy(j, y):
        xx = lax.rem(x + j, XS)
        block = wbuf.at[y, xx, whalf]
        return rcopy(block, block, wf_s.at[y, xx], wf_r.at[y, xx], sib)

    finish(0)
    finish(1)
    w_arrived()
    project(0)
    finish(2)
    project(1)
    finish(3)
    project(2)
    project(3)

    for j in range(1, PAIRS):
        p = lax.rem(pair + PAIRS - j, PAIRS)
        block = call.at[:, cap_rows(2 * p + core)]
        rcopy(block, block, cs_s.at[0], cs_r.at[p], sib).wait_recv()
        cf_copy(p).start()

    def final(rb):
        rcopy(psend.at[rb], precv.at[rb], y_s.at[rb], y_r.at[rb], sib).wait_recv()
        out_ref[rb * RB : (rb + 1) * RB, :] = (lacc[rb] + precv[rb].astype(F32)).astype(BF16)

    for rb in range(NRB):
        final(rb)
    for p in range(PAIRS):
        block = call.at[:, cap_rows(2 * p + core)]
        rcopy(block, block, cf_s.at[p], cf_r.at[p], sib).wait_recv()
    head_copy.wait()

    def normalise(i, carry):
        rows = pl.ds(pl.multiple_of(i * 32, 32), 32)
        wide = [call[kk, rows, :].astype(F32) for kk in range(KVH)]
        squares = functools.reduce(lambda a, b: a + b, [t * t for t in wide])
        mean = jnp.sum(squares, axis=1, keepdims=True) * (1.0 / (KVH * FEAT))
        r = lax.rsqrt(mean + 1e-06)
        for kk in range(KVH):
            ncap[kk, rows, :] = (wide[kk] * r * gain_ref[kk : kk + 1, :]).astype(BF16)
        return carry

    lax.fori_loop(0, NCAP // 32, normalise, 0)
    logit[...] = jnp.zeros((VOC, NCAP), F32)

    def logit_step(kk, carry):
        logit[...] += lax.dot_general(hw[:, cols(kk)], ncap[kk], NT, preferred_element_type=F32)
        return carry

    lax.fori_loop(0, KVH, logit_step, 0)
    lt = logit[...]
    ids = lax.broadcasted_iota(jnp.int32, (VOC, NCAP), 0) + (s * KVH + k) * VOC
    top = jnp.max(lt, axis=0, keepdims=True)
    st1[k, 0:1, :] = top
    st1[k, 1:2, :] = jnp.sum(jnp.exp(lt - top), axis=0, keepdims=True)
    st1[k, 2:3, :] = jnp.sum(jnp.where(ids == tgt_ref[...], lt, 0.0), axis=0, keepdims=True)

    def s1_copy(j):
        return rcopy(st1.at[k], st1.at[k], s1_s.at[j], s1_r.at[k], (s, lax.rem(k + j, KVH)))

    def s2_copy(j):
        return rcopy(st2.at[s], st2.at[s], s2_s.at[j], s2_r.at[s], (lax.rem(s + j, SEQ), k))

    def merge(blocks):
        top = jnp.max(blocks[:, 0, :], axis=0, keepdims=True)
        total = jnp.sum(blocks[:, 1, :] * jnp.exp(blocks[:, 0, :] - top), axis=0, keepdims=True)
        return top, total, jnp.sum(blocks[:, 2, :], axis=0, keepdims=True)

    for j in range(1, KVH):
        s1_copy(j).start()
    for j in range(1, KVH):
        kk = lax.rem(k + j, KVH)
        rcopy(st1.at[kk], st1.at[kk], s1_s.at[0], s1_r.at[kk], sib).wait_recv()
    top, total, target = merge(st1[...])
    st2[s, 0:1, :] = top
    st2[s, 1:2, :] = total
    st2[s, 2:3, :] = target
    for j in range(1, SEQ):
        s2_copy(j).start()
    for j in range(1, SEQ):
        ss = lax.rem(s + j, SEQ)
        rcopy(st2.at[ss], st2.at[ss], s2_s.at[0], s2_r.at[ss], sib).wait_recv()
    top, total, target = merge(st2[...])
    lp_ref[...] = target - (top + jnp.log(total))

    def wait_cq_sent(j, carry):
        cq_copy(j).wait_send()
        return carry

    def wait_cp_sent(j, carry):
        cp_copy(j).wait_send()
        return carry

    def wait_kf_sent(p, carry):
        kf_copy(p).wait_send()
        return carry

    lax.fori_loop(0, s, wait_cq_sent, 0)
    lax.fori_loop(s + 1, SEQ, wait_cp_sent, 0)
    lax.fori_loop(0, pair + 1, wait_kf_sent, 0)
    for j in range(1, PAIRS):
        pl.when(pair + j < PAIRS)(lambda j=j: kv_copy(j).wait_send())
        cs_copy(j).wait_send()
    for p in range(PAIRS):
        cf_copy(p).wait_send()
    for j in range(1, XS):
        for y in range(2):
            w_copy(j, y).wait_send()
            wf_copy(j, y).wait_send()
        for rb in range(NRB):
            a_copy(rb, j).wait_send()
    for rb in range(NRB):
        y_copy(rb).wait_send()
    for j in range(1, KVH):
        cr_copy(j).wait_send()
        ck_copy(j).wait_send()
        s1_copy(j).wait_send()
    for j in range(1, SEQ):
        s2_copy(j).wait_send()


def body(hidden_in, queries, keys, values, out_weight, norm_gain, head_weight, caption_pos, targets):
    cap_col = jnp.broadcast_to(caption_pos.reshape(SEQ, 1, CAPS), (SEQ, HEADS, CAPS)).reshape(SEQ * 64, 1)
    vmem = pl.BlockSpec(memory_space=pltpu.VMEM)
    hbm = pl.BlockSpec(memory_space=pl.ANY)
    dma = lambda *shape: pltpu.SemaphoreType.DMA(shape)
    layer_out, log_probs = pl.pallas_call(
        kernel,
        name="score_captions",
        out_shape=(
            jax.ShapeDtypeStruct((TOK, FEAT), BF16),
            jax.ShapeDtypeStruct((1, NCAP), F32),
        ),
        in_specs=[vmem, vmem, vmem, vmem, hbm, vmem, hbm, vmem, vmem],
        out_specs=(vmem, vmem),
        scratch_shapes=[
            pltpu.VMEM((PAIRS, 2 * TOK, 2 * HD), BF16),
            pltpu.VMEM((NRB * HEADS, RB, HD), F32),
            pltpu.VMEM((NRB * HEADS, RB, 2 * HD), F32),
            pltpu.VMEM((2, XS, TOK, FEAT), BF16),
            pltpu.VMEM((VOC, KVH * FEAT), BF16),
            pltpu.VMEM((KVH, NCAP, FEAT), BF16),
            pltpu.VMEM((KVH, NCAP, FEAT), BF16),
            pltpu.VMEM((NRB, XS, RB, HEADS * HD), BF16),
            pltpu.VMEM((NRB, RB, FEAT), BF16),
            pltpu.VMEM((NRB, RB, FEAT), BF16),
            pltpu.VMEM((NRB, RB, FEAT), F32),
            pltpu.VMEM((SEQ, 64, HD), BF16),
            pltpu.VMEM((SEQ, 64, 2 * HD), BF16),
            pltpu.VMEM((SEQ, 64, 2 * HD), BF16),
            pltpu.VMEM((KVH, CAPS, FEAT), BF16),
            pltpu.VMEM((KVH, CAPS, FEAT), BF16),
            pltpu.VMEM((VOC, NCAP), F32),
            pltpu.VMEM((8, NCAP), F32),
            pltpu.VMEM((KVH, 8, NCAP), F32),
            pltpu.VMEM((SEQ, 8, NCAP), F32),
            dma(KVH), dma(2), dma(1),
            dma(PAIRS), dma(PAIRS), dma(PAIRS), dma(PAIRS),
            dma(2, XS), dma(2, XS), dma(2, XS), dma(2, XS),
            dma(SEQ), dma(SEQ), dma(SEQ), dma(SEQ),
            dma(KVH), dma(KVH), dma(KVH), dma(KVH),
            dma(PAIRS), dma(PAIRS), dma(PAIRS), dma(PAIRS),
            dma(NRB, XS), dma(NRB, XS), dma(NRB), dma(NRB),
            dma(KVH), dma(KVH), dma(SEQ), dma(SEQ),
        ],
        compiler_params=pltpu.CompilerParams(
            collective_id=0, has_side_effects=True, vmem_limit_bytes=60 * 1024 * 1024
        ),
    )(
        queries, keys, values, hidden_in, out_weight, norm_gain.reshape(KVH, FEAT), head_weight,
        cap_col, targets.reshape(1, NCAP),
    )
    return layer_out, log_probs.reshape(NCAP)


def solution(mesh):
    in_specs = (
        P("seq", "kvh"),
        P("seq", "kvh"),
        P("seq", "kvh"),
        P("seq", "kvh"),
        P("kvh", None),
        P(),
        P(("seq", "kvh"), None),
        P(),
        P(),
    )
    out_specs = (P("seq", "kvh"), P())
    return jax.shard_map(body, mesh=mesh, in_specs=in_specs, out_specs=out_specs, check_vma=False)
```

time: 583 us -> 146 us (0.25)
  waiting for transfers between devices: 329 us -> 0 us
  blocking collectives: 158 us -> 0 us
  Pallas kernels: 0 us -> 138 us
  matrix products: 28.7 us -> 0 us
  loops' own time: 21.2 us -> 0 us
  local copies, waits for them, and re-layouts: 22.7 us -> 6.74 us
  between operations: 13.9 us -> 0.64 us
  other arithmetic: 7.9 us -> 0 us
    reduce_scatter x1 -> x0, waiting for transfers between devices: 211 us -> none  [body(): lax.psum_scatter(projected.astype(jnp.bfloat16), 'kvh', scatter_dimension...]
    pallas_call x0 -> x1, Pallas kernels: none -> 138 us  [body(): pl.pallas_call(kernel, name='score_captions', out_shape=(jax.ShapeDtypeSt...]
    all_gather x3 -> x0, waiting for transfers between devices: 116 us -> none  [the longest x1 42.2 us: body(): lax.all_gather(gathered, 'seq', axis=0, tiled=True).astype(jnp.float32)]
    pmax x1 -> x0, blocking collectives: 64.8 us -> none  [body(): top_logit = lax.pmax(local_max, ('seq', 'kvh'))]
    psum x1 -> x0, blocking collectives: 63.5 us -> none  [body(): exp_total, picked = lax.psum((local_total, own_target), ('seq', 'kvh'))]
    all_gather x1 -> x0, blocking collectives: 30 us -> none  [body(): gathered = lax.all_gather(caption_piece, 'kvh', axis=1, tiled=True)]
    dot_general x10 -> x0, matrix products: 28.7 us -> none  [the longest x1 10.2 us: body(): jnp.dot(attended, out_weight, preferred_element_type=jnp.float32)]
    another operation x34 -> x0, loops' own time: 21.2 us -> none  [the longest x2 20.6 us: attend(): lax.scan(step_block, states, (stacked_keys, stacked_values, jnp.arange(st...]
  transfers between devices with their start and end apart: 4 -> 0, of which waited for: 4 -> 0; matrix products, arithmetic and copies ran while one was open for 0% -> 0% of each run, Pallas kernels for 0% -> 0%
where the time goes in v1:
time: 146 us
  Pallas kernels  138 us (95%)
  local copies, waits for them, and re-layouts  6.74 us (5%)
    pallas_call x1, Pallas kernels, body(): pl.pallas_call(kernel, name='score_captions', out_shape=(jax.ShapeDtypeSt...  138 us
    unnamed x2, local copies, waits for them, and re-layouts  3.49 us

profile of v1, /device:TPU:1, one launch (start us, length us, event | category | flops | bytes accessed | tf_op | source)
XLA Modules:
  0.0 145.5 jit_solution(9852880582304155336)
XLA Ops:
  0.6 0.8 broadcast_in_dim.7
  1.4 1.4 reshape.18.gain_ref
  2.8 1.1 reshape.22.cap_ref
  3.9 138.1 %score_captions.1 = (bf16[512,1024]{1,0:T(8,128)(2,1)}, f32[1,256]{1,0:T(1,128)}) custom-call(bf16[512,512]{1,0:T(8,128)(2,1)} %q_ref.1, bf16[512,128]{1,0:T(8,128)(2,1)} %k_ref.1, bf16[512,128]{1,0:T(8,128)(2,1)} %v_ref.1, bf16[512,1024]{1,0:T(8,128)(2,1)} %hid_ref.1, bf16[512,8192]{1,0:T(8,128)(2,1)} %ow_ref.1, f32[8,1024]{1,0:T(8,128)} %reshape.18.gain_ref, ...), custom_call_target="tpu_custom_call" | custom-call | tf_op jit(solution)/shard_map/score_captions/pallas_call | solution.py:467
  142.0 2.3 %copy.14 = bf16[512,1024]{1,0:T(8,128)(2,1)} copy(bf16[512,1024]{1,0:T(8,128)(2,1)} %get-tuple-element.8) | data formatting | bytes 2097152
  144.3 1.2 copy.15
  (1 shorter events, 0.0 us)

commit v2 on v1

--- a/solution.py
+++ b/solution.py
@@ -40,17 +40,19 @@
 
 
 def kernel(
-    q_ref, k_ref, v_ref, hid_ref, ow_ref, gain_ref, hw_ref, cap_ref, tgt_ref,
+    q_ref, k_ref, v_ref, hid_ref, ow_ref, gain_ref, hw_ref, pos_ref, tgt_ref,
     out_ref, lp_ref,
     kv, m_s, acc_s, wbuf, hw, call, ncap, abuf, psend, precv, lacc,
-    cq, cpo, cpi, cro, cri, logit, stat, st1, st2,
-    wl_m, wo_m, hw_m, kv_s, kv_r, kf_s, kf_r, w_s, w_r, wf_s, wf_r,
-    cq_s, cq_r, cp_s, cp_r, cr_s, cr_r, ck_s, ck_r, cs_s, cs_r, cf_s, cf_r,
+    cap_ref, cq, cpo, cpi, cro, cri, ssq, logit, st1, st2,
+    wl_m, wo_m, hw_m, kv_s, kv_r, kf_s, kf_r, kz_s, w_s, w_r, wf_s, wf_r,
+    v_s, v_r, vf_s, vf_r, vy_s, vy_r,
+    cq_s, cq_r, cp_s, cp_r, cr_s, cr_r, ck_s, ck_r, cy_s, cy_r, cs_s, cs_r, cf_s, cf_r,
     a_s, a_r, y_s, y_r, s1_s, s1_r, s2_s, s2_r,
 ):
     s = lax.axis_index("seq")
     k = lax.axis_index("kvh")
     pair, core = lax.div(s, 2), lax.rem(s, 2)
+    ylo, z = lax.div(pair, 4), lax.rem(pair, 4)
     yhi, x = lax.div(k, XS), lax.rem(k, XS)
     other_y = 1 - yhi
     sib = (2 * pair + 1 - core, k)
@@ -67,6 +69,11 @@
 
     half = pl.ds(pl.multiple_of(core * TOK, TOK), TOK)
     whalf = pl.ds(pl.multiple_of(core * 256, 256), 256)
+    y_pair = (1 - ylo) * 4 + z
+
+    def quarter(yy):
+        return pl.ds(pl.multiple_of((yy * 2 + core) * 128, 128), 128)
+
 
     own_w = [
         pltpu.make_async_copy(ow_ref.at[:, cols(y * XS + x)], wbuf.at[y, x], wo_m.at[y])
@@ -82,17 +89,25 @@
         pl.semaphore_signal(barrier, inc=1, device_id=(lax.rem(s + j, SEQ), k), device_id_type=MESH)
     for j in range(1, KVH):
         pl.semaphore_signal(barrier, inc=1, device_id=(s, lax.rem(k + j, KVH)), device_id_type=MESH)
+    for j in range(1, KVH):
+        pl.semaphore_signal(
+            barrier, inc=1, device_id=(2 * y_pair + core, lax.rem(k + j, KVH)), device_id_type=MESH
+        )
     for c in local_w + own_w:
         c.start()
     kv[pair, half, 0:HD] = k_ref[...]
     kv[pair, half, HD : 2 * HD] = v_ref[...]
+    slot = lax.broadcasted_iota(jnp.int32, (SEQ * 64, NCAP), 0)
+    wanted = lax.div(slot, 64) * CAPS + lax.rem(slot, CAPS)
+    hit = lax.broadcasted_iota(jnp.int32, (SEQ * 64, NCAP), 1) == wanted
+    cap_ref[...] = jnp.sum(jnp.where(hit, pos_ref[...], 0), axis=1, keepdims=True)
     own_rows = pl.ds(pl.multiple_of(s * 64, 64), CAPS)
     spots = cap_ref[own_rows, :] - s * TOK
     sel = (lax.broadcasted_iota(jnp.int32, (CAPS, TOK), 1) == spots).astype(F32).astype(BF16)
     for h in range(HEADS):
         picked = jnp.dot(sel, q_ref[:, h * HD : (h + 1) * HD], preferred_element_type=F32)
         cq[s, h * CAPS : (h + 1) * CAPS, :] = picked.astype(BF16)
-    pl.semaphore_wait(barrier, SEQ - 1 + KVH - 1)
+    pl.semaphore_wait(barrier, SEQ - 1 + 2 * (KVH - 1))
 
     def cq_copy(j):
         return rcopy(cq.at[s], cq.at[s], cq_s.at[j], cq_r.at[s], (j, k))
@@ -107,13 +122,17 @@
         block = kv.at[pair, half]
         return rcopy(block, block, kv_s.at[j], kv_r.at[pair], pair_dev(pair + j))
 
+    def kz_copy(j):
+        block = kv.at[pair - 4, half]
+        return rcopy(block, block, kz_s.at[j], kv_r.at[pair - 4], pair_dev(4 + lax.rem(z + j, 4)))
+
     def kf_copy(p):
         block = kv.at[p, half]
         return rcopy(block, block, kf_s.at[p], kf_r.at[p], sib)
 
+    pl.when(ylo == 0)(lambda: kv_copy(4).start())
+    pl.when(z < 3)(lambda: kv_copy(1).start())
     kf_copy(pair).start()
-    for j in range(1, PAIRS):
-        pl.when(pair + j < PAIRS)(lambda j=j: kv_copy(j).start())
 
     def w_copy(j, y):
         xx = lax.rem(x + j, XS)
@@ -121,8 +140,8 @@
             ow_ref.at[whalf, cols(y * XS + xx)], wbuf.at[y, x, whalf], w_s.at[y, j], w_r.at[y, x], x_dev(xx)
         )
 
-    for j in range(1, XS):
-        for y in range(2):
+    for y in range(2):
+        for j in (1, 3):
             w_copy(j, y).start()
 
     ones = jnp.ones((2 * TOK, HD), BF16)
@@ -153,15 +172,18 @@
                 f = jnp.exp2((old - top) * SCALE2)
                 acc_s[at] = acc_s[at] * jnp.concatenate([f, f], axis=1) + pv
 
-    def attend_all(p, own):
-        def step(rb, carry):
-            attend(rb, p, own)
+    def attend_two(rh, p, own):
+        attend(2 * rh, p, own)
+        attend(2 * rh + 1, p, own)
+
+    def attend_all(p):
+        def step(rh, carry):
+            attend_two(rh, p, False)
             return carry
 
-        lax.fori_loop(0, NRB, step, 0)
-
-    def half_arrived(j):
-        p = pair - j
+        lax.fori_loop(0, 2, step, 0)
+
+    def half_arrived(p):
         block = kv.at[p, half]
         rcopy(block, block, kv_s.at[0], kv_r.at[p], sib).wait_recv()
         kf_copy(p).start()
@@ -170,9 +192,31 @@
         block = kv.at[p, half]
         rcopy(block, block, kf_s.at[p], kf_r.at[p], sib).wait_recv()
 
+    steps = [
+        (ylo == 1, pair - 4),
+        (z >= 1, pair - 1),
+        (ylo == 1, lax.rem(z + 3, 4)),
+        (ylo == 1, lax.rem(z + 1, 4)),
+        (ylo == 1, lax.rem(z + 2, 4)),
+        (z >= 3, pair - 3),
+        (z >= 2, pair - 2),
+    ]
+
+    def ready(i):
+        needed, p = steps[i]
+        pl.when(needed)(lambda: half_arrived(p))
+
+    def run(i):
+        needed, p = steps[i]
+
+        def work():
+            sib_arrived(p)
+            attend_all(p)
+
+        pl.when(needed)(work)
+
     sib_arrived(pair)
-    attend_all(pair, True)
-    pl.when(pair >= 1)(lambda: half_arrived(1))
+    attend_two(0, pair, True)
 
     def wait_cq(j, carry):
         rcopy(cq.at[j], cq.at[j], cq_s.at[j], cq_r.at[j], sib).wait_recv()
@@ -207,16 +251,18 @@
 
     lax.fori_loop(s + 1, SEQ, start_cp, 0)
 
-    def phase_one(j):
-        pl.when(pair >= j + 1)(lambda: half_arrived(j + 1))
-
-        def work():
-            sib_arrived(pair - j)
-            attend_all(pair - j, False)
-
-        pl.when(pair >= j)(work)
-
-    phase_one(1)
+    ready(0)
+
+    def pass_on():
+        for j in (1, 3, 2):
+            kz_copy(j).start()
+
+    pl.when(ylo == 1)(pass_on)
+    for j in (3, 2):
+        pl.when(z + j < 4)(lambda j=j: kv_copy(j).start())
+    attend_two(1, pair, True)
+    ready(1)
+    run(0)
 
     def unpack(block):
         t = block[:, HD:].astype(F32)
@@ -246,7 +292,15 @@
         cr_copy(j).start()
     head_copy.start()
 
-    phase_one(2)
+    def v_copy(y):
+        xx = lax.rem(x + 2, XS)
+        rows = quarter(ylo)
+        return rcopy(ow_ref.at[rows, cols(y * XS + xx)], wbuf.at[y, x, rows], v_s.at[y], v_r.at[y], x_dev(xx))
+
+    v_copy(0).start()
+
+    ready(2)
+    run(1)
 
     cap_sum = cro[k].astype(F32) + jnp.dot(sel, hid_ref[...], preferred_element_type=F32)
     for j in range(1, KVH):
@@ -263,48 +317,82 @@
         block = call.at[k, cap_rows(s)]
         return rcopy(block, block, ck_s.at[j], ck_r.at[k], (s, lax.rem(k + j, KVH)))
 
+    def cy_copy(j):
+        block = call.at[k, cap_rows(s)]
+        return rcopy(block, block, cy_s.at[j], cy_r.at[k], (2 * y_pair + core, lax.rem(k + j, KVH)))
+
     for j in range(1, KVH):
         ck_copy(j).start()
-
-    phase_one(3)
-
-    for j in range(1, KVH):
-        kk = lax.rem(k + j, KVH)
-        block = call.at[kk, cap_rows(s)]
-        rcopy(block, block, ck_s.at[0], ck_r.at[kk], sib).wait_recv()
-
-    def cs_copy(j):
-        block = call.at[:, cap_rows(s)]
-        return rcopy(block, block, cs_s.at[j], cs_r.at[pair], pair_dev(lax.rem(pair + j, PAIRS)))
-
-    def cf_copy(p):
-        block = call.at[:, cap_rows(2 * p + core)]
-        return rcopy(block, block, cf_s.at[p], cf_r.at[p], sib)
-
-    cf_copy(pair).start()
-    for j in range(1, PAIRS):
-        cs_copy(j).start()
-
-    for j in range(4, PAIRS):
-        if j + 1 < PAIRS:
-            pl.when(pair >= j + 1)(lambda j=j: half_arrived(j + 1))
-        pl.when(pair >= j)(lambda j=j: sib_arrived(pair - j))
+    for j in range(KVH):
+        cy_copy(j).start()
+
+    v_copy(1).start()
+
+    def wf_copy(j, y):
+        block = wbuf.at[y, lax.rem(x + j, XS), whalf]
+        return rcopy(block, block, wf_s.at[y, j], wf_r.at[y, j], sib)
+
+    for y in range(2):
+        for j in (1, 3):
+            xx = lax.rem(x + j, XS)
+            block = wbuf.at[y, xx, whalf]
+            rcopy(block, block, w_s.at[y, 0], w_r.at[y, xx], sib).wait_recv()
+            wf_copy(j, y).start()
+    ready(3)
+    run(2)
+
+    def cap_block(p, h):
+        return call.at[4 * h : 4 * h + 4, cap_rows(2 * p + core)]
+
+    def cs_copy(h, j, p):
+        block = cap_block(p, h)
+        peer = ylo * 4 + lax.rem(z + j, 4)
+        return rcopy(block, block, cs_s.at[h, lax.div(p, 4) * 4 + j], cs_r.at[h, p], pair_dev(peer))
+
+    def cf_copy(h, p):
+        block = cap_block(p, h)
+        return rcopy(block, block, cf_s.at[h, p], cf_r.at[h, p], sib)
+
+    def spread():
+        for j in range(1, KVH):
+            kk = lax.rem(k + j, KVH)
+            block = call.at[kk, cap_rows(s)]
+            rcopy(block, block, ck_s.at[0], ck_r.at[kk], sib).wait_recv()
+        for kk in range(KVH):
+            block = call.at[kk, cap_rows(2 * y_pair + core)]
+            rcopy(block, block, ck_s.at[0], cy_r.at[kk], sib).wait_recv()
+        for h in range(2):
+            for j in (1, 3, 2):
+                for p in (pair, y_pair):
+                    cs_copy(h, j, p).start()
+            for p in (pair, y_pair):
+                cf_copy(h, p).start()
+
+    def cap_arrived(h, p):
+        block = cap_block(p, h)
+        rcopy(block, block, cs_s.at[h, 0], cs_r.at[h, p], sib).wait_recv()
+        cf_copy(h, p).start()
 
     def a_copy(rb, j):
         block = abuf.at[rb, x]
         return rcopy(block, block, a_s.at[rb, j], a_r.at[rb, x], x_dev(lax.rem(x + j, XS)))
 
-    def finish(rb):
-        def step(j, carry):
-            attend(rb, pair - j, False)
-            return carry
-
-        lax.fori_loop(4, pair + 1, step, 0)
-        for h in range(HEADS):
-            done = acc_s[rb * HEADS + h]
-            abuf[rb, x, :, h * HD : (h + 1) * HD] = (done[:, :HD] / done[:, HD:]).astype(BF16)
-        for j in range(1, XS):
-            a_copy(rb, j).start()
+    def finish(rh):
+        for i in (4, 5, 6):
+            needed, p = steps[i]
+
+            def work():
+                if rh == 0:
+                    sib_arrived(p)
+                attend_two(rh, p, False)
+
+            pl.when(needed)(work)
+        for rb in (2 * rh, 2 * rh + 1):
+            for h in range(HEADS):
+                done = acc_s[rb * HEADS + h]
+                abuf[rb, x, :, h * HD : (h + 1) * HD] = (done[:, :HD] / done[:, HD:]).astype(BF16)
+            for j in (1, 3, 2):
+                a_copy(rb, j).start()
 
     def y_copy(rb):
         return rcopy(psend.at[rb], precv.at[rb], y_s.at[rb], y_r.at[rb], y_dev)
@@ -323,72 +411,93 @@
         y_copy(rb).start()
         lacc[rb] = product(yhi) + hid_ref[rb * RB : (rb + 1) * RB, :].astype(F32)
 
+    x_two = lax.rem(x + 2, XS)
+
+    def vf_copy(y, yy):
+        block = wbuf.at[y, x_two, quarter(yy)]
+        return rcopy(block, block, vf_s.at[y, yy], vf_r.at[y, yy], sib)
+
+    def vy_copy(y):
+        block = wbuf.at[y, x_two, quarter(ylo)]
+        return rcopy(block, block, vy_s.at[y], vy_r.at[y], pair_dev(y_pair))
+
+    def v_arrived(y):
+        block = wbuf.at[y, x_two, quarter(ylo)]
+        rcopy(block, block, v_s.at[0], v_r.at[y], sib).wait_recv()
+        vy_copy(y).start()
+        vf_copy(y, ylo).start()
+
     def w_arrived():
         for c in own_w:
             c.wait()
-        for j in range(1, XS):
-            xx = lax.rem(x + j, XS)
-            for y in range(2):
-                block = wbuf.at[y, xx, whalf]
-                rcopy(block, block, w_s.at[y, 0], w_r.at[y, xx], sib).wait_recv()
-                wf_copy(j, y).start()
-        for j in range(1, XS):
-            xx = lax.rem(x + j, XS)
-            for y in range(2):
-                block = wbuf.at[y, xx, whalf]
-                rcopy(block, block, wf_s.at[y, xx], wf_r.at[y, xx], sib).wait_recv()
-
-    def wf_copy(j, y):
-        xx = lax.rem(x + j, XS)
-        block = wbuf.at[y, xx, whalf]
-        return rcopy(block, block, wf_s.at[y, xx], wf_r.at[y, xx], sib)
-
+        for y in range(2):
+            block = wbuf.at[y, x_two, quarter(1 - ylo)]
+            rcopy(block, block, v_s.at[0], vy_r.at[y], sib).wait_recv()
+            vf_copy(y, 1 - ylo).start()
+        for y in range(2):
+            for j in (1, 3):
+                block = wbuf.at[y, lax.rem(x + j, XS), whalf]
+                rcopy(block, block, wf_s.at[y, 0], wf_r.at[y, j], sib).wait_recv()
+            for yy in range(2):
+                block = wbuf.at[y, x_two, quarter(yy)]
+                rcopy(block, block, v_s.at[0], vf_r.at[y, yy], sib).wait_recv()
+
+    spread()
+    v_arrived(0)
+    ready(4)
+    run(3)
+    ready(5)
+    ready(6)
     finish(0)
+    v_arrived(1)
     finish(1)
     w_arrived()
     project(0)
-    finish(2)
     project(1)
-    finish(3)
-    project(2)
-    project(3)
-
-    for j in range(1, PAIRS):
-        p = lax.rem(pair + PAIRS - j, PAIRS)
-        block = call.at[:, cap_rows(2 * p + core)]
-        rcopy(block, block, cs_s.at[0], cs_r.at[p], sib).wait_recv()
-        cf_copy(p).start()
+
+    def scale(h, p):
+        block = cap_block(p, h)
+        rcopy(block, block, cf_s.at[h, p], cf_r.at[h, p], sib).wait_recv()
+        rows = pl.ds(pl.multiple_of(p * 32, 32), 32)
+        wide = [call[kk, rows, :].astype(F32) for kk in range(4 * h, 4 * h + 4)]
+        squares = functools.reduce(lambda a, b: a + b, [t * t for t in wide])
+        part = jnp.sum(squares, axis=1, keepdims=True)
+        ssq[rows, :] = part if h == 0 else ssq[rows, :] + part
+        for kk in range(4):
+            at = 4 * h + kk
+            gain = gain_ref[:, at * FEAT : (at + 1) * FEAT]
+            ncap[at, rows, :] = (wide[kk] * gain).astype(BF16)
+
+    def take(h):
+        last = pair
+        for j in (1, 5, 3, 7, 2, 6):
+            p = lax.rem(ylo + j // 4, 2) * 4 + lax.rem(z + j, 4)
+            cap_arrived(h, p)
+            scale(h, last)
+            last = p
+        scale(h, y_pair)
+        scale(h, last)
+
+    def half_logits(h):
+        parts = [
+            lax.dot_general(hw[:, kk * FEAT : (kk + 1) * FEAT], ncap[kk], NT, preferred_element_type=F32)
+            for kk in range(4 * h, 4 * h + 4)
+        ]
+        return (parts[0] + parts[1]) + (parts[2] + parts[3])
 
     def final(rb):
         rcopy(psend.at[rb], precv.at[rb], y_s.at[rb], y_r.at[rb], sib).wait_recv()
         out_ref[rb * RB : (rb + 1) * RB, :] = (lacc[rb] + precv[rb].astype(F32)).astype(BF16)
 
-    for rb in range(NRB):
-        final(rb)
-    for p in range(PAIRS):
-        block = call.at[:, cap_rows(2 * p + core)]
-        rcopy(block, block, cf_s.at[p], cf_r.at[p], sib).wait_recv()
+    take(0)
     head_copy.wait()
-
-    def normalise(i, carry):
-        rows = pl.ds(pl.multiple_of(i * 32, 32), 32)
-        wide = [call[kk, rows, :].astype(F32) for kk in range(KVH)]
-        squares = functools.reduce(lambda a, b: a + b, [t * t for t in wide])
-        mean = jnp.sum(squares, axis=1, keepdims=True) * (1.0 / (KVH * FEAT))
-        r = lax.rsqrt(mean + 1e-06)
-        for kk in range(KVH):
-            ncap[kk, rows, :] = (wide[kk] * r * gain_ref[kk : kk + 1, :]).astype(BF16)
-        return carry
-
-    lax.fori_loop(0, NCAP // 32, normalise, 0)
-    logit[...] = jnp.zeros((VOC, NCAP), F32)
-
-    def logit_step(kk, carry):
-        logit[...] += lax.dot_general(hw[:, cols(kk)], ncap[kk], NT, preferred_element_type=F32)
-        return carry
-
-    lax.fori_loop(0, KVH, logit_step, 0)
-    lt = logit[...]
+    logit[...] = half_logits(0)
+    project(2)
+    take(1)
+    square = (NCAP, NCAP)
+    diagonal = lax.broadcasted_iota(jnp.int32, square, 0) == lax.broadcasted_iota(jnp.int32, square, 1)
+    mean = jnp.sum(jnp.where(diagonal, ssq[...], 0.0), axis=0, keepdims=True) * (1.0 / (KVH * FEAT))
+    lt = (logit[...] + half_logits(1)) * lax.rsqrt(mean + 1e-06)
     ids = lax.broadcasted_iota(jnp.int32, (VOC, NCAP), 0) + (s * KVH + k) * VOC
     top = jnp.max(lt, axis=0, keepdims=True)
     st1[k, 0:1, :] = top
@@ -408,6 +517,7 @@
 
     for j in range(1, KVH):
         s1_copy(j).start()
+    project(3)
     for j in range(1, KVH):
         kk = lax.rem(k + j, KVH)
         rcopy(st1.at[kk], st1.at[kk], s1_s.at[0], s1_r.at[kk], sib).wait_recv()
@@ -417,6 +527,8 @@
     st2[s, 2:3, :] = target
     for j in range(1, SEQ):
         s2_copy(j).start()
+    for rb in range(NRB):
+        final(rb)
     for j in range(1, SEQ):
         ss = lax.rem(s + j, SEQ)
         rcopy(st2.at[ss], st2.at[ss], s2_s.at[0], s2_r.at[ss], sib).wait_recv()
@@ -438,29 +550,39 @@
     lax.fori_loop(0, s, wait_cq_sent, 0)
     lax.fori_loop(s + 1, SEQ, wait_cp_sent, 0)
     lax.fori_loop(0, pair + 1, wait_kf_sent, 0)
-    for j in range(1, PAIRS):
-        pl.when(pair + j < PAIRS)(lambda j=j: kv_copy(j).wait_send())
-        cs_copy(j).wait_send()
-    for p in range(PAIRS):
-        cf_copy(p).wait_send()
-    for j in range(1, XS):
-        for y in range(2):
+    pl.when(ylo == 0)(lambda: kv_copy(4).wait_send())
+    for j in range(1, 4):
+        pl.when(z + j < 4)(lambda j=j: kv_copy(j).wait_send())
+        pl.when(ylo == 1)(lambda j=j: kz_copy(j).wait_send())
+    for h in range(2):
+        for j in range(1, 4):
+            for p in (pair, y_pair):
+                cs_copy(h, j, p).wait_send()
+        for p in range(PAIRS):
+            cf_copy(h, p).wait_send()
+    for y in range(2):
+        for j in (1, 3):
             w_copy(j, y).wait_send()
             wf_copy(j, y).wait_send()
-        for rb in range(NRB):
+        v_copy(y).wait_send()
+        vy_copy(y).wait_send()
+        for yy in range(2):
+            vf_copy(y, yy).wait_send()
+    for rb in range(NRB):
+        for j in range(1, XS):
             a_copy(rb, j).wait_send()
-    for rb in range(NRB):
         y_copy(rb).wait_send()
+    cy_copy(0).wait_send()
     for j in range(1, KVH):
         cr_copy(j).wait_send()
         ck_copy(j).wait_send()
+        cy_copy(j).wait_send()
         s1_copy(j).wait_send()
     for j in range(1, SEQ):
         s2_copy(j).wait_send()
 
 
 def body(hidden_in, queries, keys, values, out_weight, norm_gain, head_weight, caption_pos, targets):
-    cap_col = jnp.broadcast_to(caption_pos.reshape(SEQ, 1, CAPS), (SEQ, HEADS, CAPS)).reshape(SEQ * 64, 1)
     vmem = pl.BlockSpec(memory_space=pltpu.VMEM)
     hbm = pl.BlockSpec(memory_space=pl.ANY)
     dma = lambda *shape: pltpu.SemaphoreType.DMA(shape)
@@ -485,21 +607,23 @@
             pltpu.VMEM((NRB, RB, FEAT), BF16),
             pltpu.VMEM((NRB, RB, FEAT), BF16),
             pltpu.VMEM((NRB, RB, FEAT), F32),
+            pltpu.VMEM((SEQ * 64, 1), jnp.int32),
             pltpu.VMEM((SEQ, 64, HD), BF16),
             pltpu.VMEM((SEQ, 64, 2 * HD), BF16),
             pltpu.VMEM((SEQ, 64, 2 * HD), BF16),
             pltpu.VMEM((KVH, CAPS, FEAT), BF16),
             pltpu.VMEM((KVH, CAPS, FEAT), BF16),
+            pltpu.VMEM((NCAP, 1), F32),
             pltpu.VMEM((VOC, NCAP), F32),
-            pltpu.VMEM((8, NCAP), F32),
             pltpu.VMEM((KVH, 8, NCAP), F32),
             pltpu.VMEM((SEQ, 8, NCAP), F32),
             dma(KVH), dma(2), dma(1),
-            dma(PAIRS), dma(PAIRS), dma(PAIRS), dma(PAIRS),
+            dma(PAIRS), dma(PAIRS), dma(PAIRS), dma(PAIRS), dma(XS),
             dma(2, XS), dma(2, XS), dma(2, XS), dma(2, XS),
+            dma(2), dma(2), dma(2, 2), dma(2, 2), dma(2), dma(2),
             dma(SEQ), dma(SEQ), dma(SEQ), dma(SEQ),
-            dma(KVH), dma(KVH), dma(KVH), dma(KVH),
-            dma(PAIRS), dma(PAIRS), dma(PAIRS), dma(PAIRS),
+            dma(KVH), dma(KVH), dma(KVH), dma(KVH), dma(KVH), dma(KVH),
+            dma(2, PAIRS), dma(2, PAIRS), dma(2, PAIRS), dma(2, PAIRS),
             dma(NRB, XS), dma(NRB, XS), dma(NRB), dma(NRB),
             dma(KVH), dma(KVH), dma(SEQ), dma(SEQ),
         ],
@@ -507,8 +631,8 @@
             collective_id=0, has_side_effects=True, vmem_limit_bytes=60 * 1024 * 1024
         ),
     )(
-        queries, keys, values, hidden_in, out_weight, norm_gain.reshape(KVH, FEAT), head_weight,
-        cap_col, targets.reshape(1, NCAP),
+        queries, keys, values, hidden_in, out_weight, norm_gain.reshape(1, KVH * FEAT), head_weight,
+        caption_pos.reshape(1, NCAP), targets.reshape(1, NCAP),
     )
     return layer_out, log_probs.reshape(NCAP)
 

time: 146 us -> 110 us (0.75)
  Pallas kernels: 138 us -> 106 us
  local copies, waits for them, and re-layouts: 6.74 us -> 3.5 us
    pallas_call x1, Pallas kernels: 138 us -> 106 us  [body(): pl.pallas_call(kernel, name='score_captions', out_shape=(jax.ShapeDtypeSt...]
    reshape x2 -> x0, local copies, waits for them, and re-layouts: 2.49 us -> none  [the longest x1 1.39 us: body(): norm_gain.reshape(KVH, FEAT)]
where the time goes in v2:
time: 110 us
  Pallas kernels  106 us (96%)
  local copies, waits for them, and re-layouts  3.5 us (3%)
    pallas_call x1, Pallas kernels, body(): pl.pallas_call(kernel, name='score_captions', out_shape=(jax.ShapeDtypeSt...  106 us
    unnamed x2, local copies, waits for them, and re-layouts  3.5 us

profile of v2, /device:TPU:1, one launch (start us, length us, event | category | flops | bytes accessed | tf_op | source)
XLA Modules:
  0.0 110.1 jit_solution(6575180585393897110)
XLA Ops:
  0.6 105.9 %score_captions.1 = (bf16[512,1024]{1,0:T(8,128)(2,1)}, f32[1,256]{1,0:T(1,128)}) custom-call(bf16[512,512]{1,0:T(8,128)(2,1)} %q_ref.1, bf16[512,128]{1,0:T(8,128)(2,1)} %k_ref.1, bf16[512,128]{1,0:T(8,128)(2,1)} %v_ref.1, bf16[512,1024]{1,0:T(8,128)(2,1)} %hid_ref.1, bf16[512,8192]{1,0:T(8,128)(2,1)} %ow_ref.1, f32[1,8192]{1,0:T(1,128)} %bitcast.4, ...), custom_call_target="tpu_custom_call" | custom-call | tf_op jit(solution)/shard_map/score_captions/pallas_call | solution.py:589
  106.6 2.3 %copy.13 = bf16[512,1024]{1,0:T(8,128)(2,1)} copy(bf16[512,1024]{1,0:T(8,128)(2,1)} %get-tuple-element.8) | data formatting | bytes 2097152
  108.8 1.2 %copy.14 = f32[256]{0:T(256)} copy(f32[256]{0:T(256)} %bitcast.7) | data formatting | bytes 2048
